TPU v7x, 128 devices: a whole 4x4x4 slice. The times are simulated.
128 devices in a mesh: member: 8 (over y_lo, z), space: 16 (over y_hi, x, core).
Axes of the slice: x: 4, y: 4 (y_hi: 2, y_lo: 2; y = y_hi * 2 + y_lo), z: 4, core: 2. Of those that a mesh axis runs over, the one named last changes fastest.
Arguments:
- latent_state: bfloat16 [64, 128, 640], P('space'), may hold values from -6 to 6
- member_noise: bfloat16 [16, 64, 128, 640], P('member', 'space'), may hold values from -6 to 6
- conv_weight: float32 [9, 640], replicated, may hold values from -2 to 2
- norm_gain: float32 [640], replicated, may hold values from 0.1 to 1.9
- weight_in: bfloat16 [1920, 640], replicated, may hold values from -0.25 to 0.25
- weight_down: bfloat16 [1920, 640], replicated, may hold values from -0.125 to 0.125
- weight_head: bfloat16 [640, 320], replicated, may hold values from -0.25 to 0.25
- target_field: float32 [64, 128, 320], P('space'), may hold values from -6 to 6
Outputs:
- grad_in: float32 [1920, 640], P(('member', 'space'))
- grad_down: float32 [1920, 640], P(('member', 'space'))
- grad_head: float32 [640, 320], replicated
- grad_gain: float32 [640], replicated
- grad_conv: float32 [9, 640], replicated
All inputs are finite; a program needn't handle non-finite values.
Results may differ from a plain program's by a relative error of at most 0.007.
Values may be sent and summed in bfloat16 or wider, within the bound.
A program may use at most 128 MiB of HBM per device.

v0:
```python
import functools
import math

import jax
import jax.numpy as jnp
from jax import lax
from jax.experimental import pallas as pl
from jax.experimental.pallas import tpu as pltpu
from jax.sharding import PartitionSpec as P

BF = jnp.bfloat16
F32 = jnp.float32
MESH = pl.DeviceIdType.MESH

MEM = 2
LATD = 4
LON = 128
D = 640
OUTC = 320
FFR = 1920
FF = 2048
ROWS = MEM * LON
MEMBERS = 16
POINTS = 8192
SCALE = math.sqrt(MEMBERS * OUTC / POINTS)
GC = math.sqrt(2.0 / math.pi)
GROUP = [(dz, dy) for dz in range(4) for dy in range(2)][1:]
CHUNKS = [
    ("down", 512, 128, "zxy"),
    ("down", 0, 256, "xyz"),
    ("down", 256, 256, "yzx"),
    ("in", 0, 256, "xyz"),
    ("in", 256, 256, "yzx"),
    ("in", 512, 128, "zxy"),
]
WIDTH = [256, 256, 256, 256, 256, 128]
HEAD_TILES = 120


def dot(a, b, ca, cb):
    return lax.dot_general(a, b, (((ca,), (cb,)), ((), ())), preferred_element_type=F32)


def scratch():
    out = {
        "noise": pltpu.VMEM((LATD, MEM, LON, D), BF),
        "latent": pltpu.VMEM((LATD, LON, D), BF),
        "wraw": pltpu.VMEM((FFR, D), BF),
        "win": pltpu.VMEM((FF, D), BF),
        "wdn": pltpu.VMEM((FF, D), BF),
        "whd": pltpu.VMEM((D, OUTC), BF),
        "tgt": pltpu.VMEM((LATD, 16, OUTC), F32),
        "mixed": pltpu.VMEM((LATD + 2, MEM, LON, D), BF),
        "cbuf": pltpu.VMEM((ROWS, D), F32),
        "normal": pltpu.VMEM((LATD, ROWS, D), F32),
        "istd": pltpu.VMEM((LATD, ROWS, 128), F32),
        "normed": pltpu.VMEM((LATD * ROWS, D), BF),
        "slope": pltpu.VMEM((LATD * ROWS, FF), F32),
        "activ": pltpu.VMEM((LATD * ROWS, FF), BF),
        "gpre": pltpu.VMEM((LATD * ROWS, FF), BF),
        "hidden": pltpu.VMEM((LATD * ROWS, D), BF),
        "ghid": pltpu.VMEM((LATD * ROWS, D), BF),
        "ysend": pltpu.VMEM((LATD, MEM, LON, OUTC), BF),
        "yrecv": pltpu.VMEM((LATD, MEMBERS, 16, OUTC), BF),
        "gsend": pltpu.VMEM((LATD, MEMBERS, 16, OUTC), BF),
        "grecv": pltpu.VMEM((LATD, MEM, LON, OUTC), BF),
        "cacc": pltpu.VMEM((10, 8, D), F32),
        "hall": pltpu.VMEM((2, 4, 4, 4, 16, 128), F32),
        "arc": pltpu.VMEM((2, 10, D), F32),
        "arx": pltpu.VMEM((4, 10, D), F32),
        "ary": pltpu.VMEM((4, 10, D), F32),
        "arz": pltpu.VMEM((4, 10, D), F32),
        "l_sem": pltpu.SemaphoreType.DMA((LATD + 5,)),
        "h_ss": pltpu.SemaphoreType.DMA((2,)),
        "h_rs": pltpu.SemaphoreType.DMA((2,)),
        "y_ss": pltpu.SemaphoreType.DMA((LATD, 7)),
        "y_rs": pltpu.SemaphoreType.DMA((LATD, 7)),
        "g_ss": pltpu.SemaphoreType.DMA((LATD, 7)),
        "g_rs": pltpu.SemaphoreType.DMA((LATD, 7)),
        "r_ss": pltpu.SemaphoreType.DMA((6, 10)),
        "r_rs": pltpu.SemaphoreType.DMA((6, 10)),
        "ag_ss": pltpu.SemaphoreType.DMA((10,)),
        "ag_rs": pltpu.SemaphoreType.DMA((10,)),
        "ar_ss": pltpu.SemaphoreType.DMA((10,)),
        "ar_rs": pltpu.SemaphoreType.DMA((10,)),
    }
    for k, w in enumerate(WIDTH):
        out[f"T{k}"] = pltpu.VMEM((2, 4, 4, 4, 16, w), BF)
        out[f"Ra{k}"] = pltpu.VMEM((4, 4, 4, 16, w), BF)
        out[f"Sb{k}"] = pltpu.VMEM((3, 4, 4, 16, w), BF)
        out[f"Rb{k}"] = pltpu.VMEM((3, 4, 4, 16, w), BF)
        out[f"Sc{k}"] = pltpu.VMEM((4, 4, 16, w), F32)
        out[f"Rc{k}"] = pltpu.VMEM((3, 4, 16, w), F32)
        out[f"Sd{k}"] = pltpu.VMEM((4, 16, w), F32)
        out[f"Rd{k}"] = pltpu.VMEM((3, 16, w), F32)
    return out


NAMES = list(scratch())


def kernel(
    lat_hbm, noise_hbm, cw_ref, gain_ref, win_hbm, wdn_hbm, whd_hbm, tgt_hbm,
    gin_out, gdn_out, head_out, gain_out, conv_out, *refs,
):
    s = dict(zip(NAMES, refs))
    member = lax.axis_index("member")
    space = lax.axis_index("space")
    ylo, z = member // 4, member % 4
    yhi, x, core = space // 8, (space // 2) % 4, space % 2
    y = yhi * 2 + ylo
    at = {"x": x, "y": y, "z": z, "c": core}

    def place(x_, y_, z_, c_):
        return ((y_ % 2) * 4 + z_, (y_ // 2) * 8 + x_ * 2 + c_)

    def partner(axis, step):
        c = dict(at)
        size = 2 if axis == "c" else 4
        c[axis] = (c[axis] + step) % size
        return place(c["x"], c["y"], c["z"], c["c"])

    def mate(dz, dy):
        return ((ylo + dy) % 2) * 4 + (z + dz) % 4

    def halo(step):
        return (member, (space + step) % 16)

    def remote(src, dst, ss, rs, dev):
        return pltpu.make_async_remote_copy(
            src_ref=src, dst_ref=dst, send_sem=ss, recv_sem=rs, device_id=dev, device_id_type=MESH
        )

    barrier = pltpu.get_barrier_semaphore()
    friends = [(mate(dz, dy), space) for dz, dy in GROUP]
    friends += [partner("c", 1), halo(1), halo(-1)]
    friends += [partner(a, j) for a in "xy" for j in (1, 2, 3)]
    for dev in friends:
        pl.semaphore_signal(barrier, inc=1, device_id=dev, device_id_type=MESH)

    lsem = s["l_sem"]
    lat_cp = pltpu.make_async_copy(lat_hbm, s["latent"], lsem.at[LATD])
    noise_cp = [
        pltpu.make_async_copy(noise_hbm.at[:, i], s["noise"].at[i], lsem.at[i]) for i in range(LATD)
    ]
    win_cp = pltpu.make_async_copy(win_hbm, s["wraw"], lsem.at[LATD + 1])
    wdn_cp = pltpu.make_async_copy(wdn_hbm, s["wraw"], lsem.at[LATD + 2])
    whd_cp = pltpu.make_async_copy(whd_hbm, s["whd"], lsem.at[LATD + 3])
    mine16 = pl.ds(pl.multiple_of(member * 16, 16), 16)
    tgt_cp = pltpu.make_async_copy(tgt_hbm.at[:, mine16], s["tgt"], lsem.at[LATD + 4])
    lat_cp.start()
    for i in (0, 3, 1, 2):
        noise_cp[i].start()
    win_cp.start()
    whd_cp.start()
    tgt_cp.start()

    mixed = s["mixed"]

    def mix(i):
        noise_cp[i].wait()
        base = s["latent"][i].astype(F32)
        for m in range(MEM):
            mixed[i + 1, m] = (base + s["noise"][i, m].astype(F32)).astype(BF)

    halo_cp = [
        remote(mixed.at[1], mixed.at[5], s["h_ss"].at[0], s["h_rs"].at[0], halo(-1)),
        remote(mixed.at[4], mixed.at[0], s["h_ss"].at[1], s["h_rs"].at[1], halo(1)),
    ]
    lat_cp.wait()
    mix(0)
    mix(3)
    pl.semaphore_wait(barrier, len(friends))
    for cp in halo_cp:
        cp.start()
    mix(1)
    mix(2)

    row_at = lax.broadcasted_iota(jnp.int32, (256, 240), 0)
    col_at = lax.broadcasted_iota(jnp.int32, (256, 240), 1)
    spread = jnp.where(
        (row_at % 16 < 15) & (col_at == (row_at // 16) * 15 + row_at % 16), 1.0, 0.0
    ).astype(BF)

    def pad_rows(dst):
        for b in range(8):
            dst[256 * b : 256 * b + 256, :] = dot(
                spread, s["wraw"][240 * b : 240 * b + 240, :], 1, 0
            ).astype(BF)

    win_cp.wait()
    pad_rows(s["win"])
    wdn_cp.start()
    s["cacc"][...] = jnp.zeros((10, 8, D), F32)
    wdn_cp.wait()
    pad_rows(s["wdn"])
    whd_cp.wait()
    tgt_cp.wait()

    def y_copy(ci, k):
        dz, dy = GROUP[k]
        to = mate(dz, dy)
        return remote(
            s["ysend"].at[ci, :, pl.ds(pl.multiple_of(to * 16, 16), 16)],
            s["yrecv"].at[ci, pl.ds(member * 2, 2)],
            s["y_ss"].at[ci, k], s["y_rs"].at[ci, k], (to, space),
        )

    def g_copy(ci, k):
        dz, dy = GROUP[k]
        to = mate(dz, dy)
        return remote(
            s["gsend"].at[ci, pl.ds(to * 2, 2)],
            s["grecv"].at[ci, :, mine16],
            s["g_ss"].at[ci, k], s["g_rs"].at[ci, k], (to, space),
        )

    gain = gain_ref[...]

    def forward(ci):
        i = (ci + 1) % LATD
        r0 = pl.multiple_of(ci * ROWS, ROWS)
        rows = pl.ds(r0, ROWS)
        for m in range(MEM):
            for lt in range(D // 128):
                lanes = slice(lt * 128, lt * 128 + 128)
                part = [None] * 3
                for a in range(3):
                    cells = mixed[i + a, m, :, lanes].astype(F32)
                    for b in range(3):
                        term = cw_ref[3 * a + b : 3 * a + b + 1, lanes] * cells
                        part[b] = term if a == 0 else part[b] + term
                s["cbuf"][m * LON : (m + 1) * LON, lanes] = (
                    part[1] + pltpu.roll(part[0], 1, 0) + pltpu.roll(part[2], LON - 1, 0)
                )
        for q in range(ROWS // 32):
            here = slice(q * 32, q * 32 + 32)
            conv = s["cbuf"][here, :]
            center = conv - jnp.mean(conv, axis=-1, keepdims=True)
            inv = lax.rsqrt(jnp.mean(center * center, axis=-1, keepdims=True) + 1e-05)
            normal = center * inv
            s["normal"][ci, here, :] = normal
            s["istd"][ci, here, :] = jnp.broadcast_to(inv, (32, 128))
            s["normed"][pl.ds(pl.multiple_of(r0 + q * 32, 32), 32), :] = (normal * gain).astype(BF)
        normed = s["normed"][rows, :]
        for f in range(4):
            cols = slice(f * 512, f * 512 + 512)
            pre = dot(normed, s["win"][cols, :], 1, 1)
            sq = pre * pre
            t = jnp.tanh(pre * (GC + (GC * 0.044715) * sq))
            half = 0.5 + 0.5 * t
            act = pre * half
            s["activ"][rows, cols] = act.astype(BF)
            s["slope"][rows, cols] = half + act * (1.0 - t) * (GC + (3 * GC * 0.044715) * sq)
        down = dot(s["activ"][rows, :], s["wdn"][...], 1, 0)
        base = mixed[i + 1].reshape(ROWS, D).astype(F32)
        hidden = (base + down).astype(BF)
        s["hidden"][rows, :] = hidden
        pred = dot(hidden, s["whd"][...], 1, 0)
        s["ysend"][ci] = pred.astype(BF).reshape(MEM, LON, OUTC)
        s["yrecv"][ci, pl.ds(member * 2, 2)] = s["ysend"][ci, :, mine16]
        for k in range(7):
            y_copy(ci, k).start()

    def score(ci):
        i = (ci + 1) % LATD
        for k in range(7):
            y_copy(ci, k).wait_recv()
        yb = s["yrecv"][ci].reshape(256, OUTC)
        gram = dot(yb, yb, 1, 1)
        r = lax.broadcasted_iota(jnp.int32, (256, 256), 0)
        c = lax.broadcasted_iota(jnp.int32, (256, 256), 1)
        diag = jnp.where(r == c, gram, 0.0)
        sq_r = jnp.sum(diag, axis=1, keepdims=True)
        sq_c = jnp.sum(diag, axis=0, keepdims=True)
        inv = lax.rsqrt(jnp.maximum(sq_r + sq_c - 2.0 * gram + 1.0, 1.0))
        w = jnp.where(r % 16 == c % 16, inv, 0.0).astype(BF)
        w_sum = jnp.sum(w.astype(F32), axis=1, keepdims=True)
        pulled = dot(w, yb, 1, 0)
        yf = yb.astype(F32)
        err = (yf.reshape(16, 16, OUTC) - s["tgt"][i][None]).reshape(256, OUTC)
        far = lax.rsqrt(jnp.sum(err * err, axis=-1, keepdims=True) + 1.0)
        grad = err * (far * (SCALE / MEMBERS)) - (yf * w_sum - pulled) * (
            SCALE / (MEMBERS * (MEMBERS - 1))
        )
        s["gsend"][ci] = grad.astype(BF).reshape(MEMBERS, 16, OUTC)
        s["grecv"][ci, :, mine16] = s["gsend"][ci, pl.ds(member * 2, 2)]
        for k in range(7):
            g_copy(ci, k).start()

    @pl.loop(0, LATD)
    def _(ci):
        @pl.when(ci == 2)
        def _():
            for cp in halo_cp:
                cp.wait()

            @pl.when(space == 0)
            def _():
                mixed[0] = jnp.zeros((MEM, LON, D), BF)

            @pl.when(space == 15)
            def _():
                mixed[5] = jnp.zeros((MEM, LON, D), BF)

        forward(ci)

        @pl.when(ci > 0)
        def _():
            score(ci - 1)

    def order(k):
        return CHUNKS[k][3]

    def rs_copy(k, stage, j=1):
        o = order(k)
        if stage == 0:
            n, src, dst, dev = 0, s[f"T{k}"].at[1 - core], s[f"Ra{k}"], partner("c", 1)
        else:
            pair = {1: ("Sb", "Rb"), 2: ("Sc", "Rc"), 3: ("Sd", "Rd")}[stage]
            n = 3 * (stage - 1) + j
            src, dst = s[f"{pair[0]}{k}"].at[j - 1], s[f"{pair[1]}{k}"].at[j - 1]
            dev = partner(o[stage - 1], j)
        return remote(src, dst, s["r_ss"].at[k, n], s["r_rs"].at[k, n], dev)

    def spot(k, o_ylo, o_z, o_yhi, o_x):
        v = {"x": o_x, "y": o_yhi * 2 + o_ylo, "z": o_z}
        return tuple(v[a] for a in order(k))

    def product(k, left, right):
        _, c0, w, _ = CHUNKS[k]
        T = s[f"T{k}"]

        @pl.loop(0, 2)
        def _(o_ylo):
            half = dot(
                left[:, pl.ds(pl.multiple_of(o_ylo * 1024, 1024), 1024)], right[:, c0 : c0 + w], 0, 0
            ).astype(BF)
            for g in range(64):
                o_z, o_yhi, o_x, o_c = g // 16, (g // 8) % 2, (g // 2) % 4, g % 2
                i1, i2, i3 = spot(k, o_ylo, o_z, o_yhi, o_x)
                T[o_c, i1, i2, i3, :, 0:w] = half[g * 16 : g * 16 + 16, :]

    def head_product(k):
        T = s[f"T{k}"]
        grad = dot(s["hidden"][...], s["grecv"][...].reshape(LATD * ROWS, OUTC), 0, 0).astype(BF)
        for t in range(128):
            i1, i2, i3 = spot(k, t // 64, (t // 16) % 4, (t // 8) % 2, (t // 2) % 4)
            at_ = (t % 2, i1, i2, i3)
            if t >= HEAD_TILES:
                T[(*at_, slice(None), slice(128, 256))] = jnp.zeros((16, 128), BF)
                continue
            rt, ct = t // 3, t % 3
            tile = grad[rt * 16 : rt * 16 + 16, ct * 128 : min(OUTC, ct * 128 + 128)]
            if ct == 2:
                T[(*at_, slice(None), slice(192, 256))] = jnp.zeros((16, 64), BF)
            T[(*at_, slice(None), slice(128, 128 + tile.shape[1]))] = tile

    def stage1(k):
        a1 = at[order(k)[0]]
        T, Ra, Sb = s[f"T{k}"], s[f"Ra{k}"], s[f"Sb{k}"]
        rs_copy(k, 0).wait_recv()
        for j in (1, 2, 3):
            n = (a1 + j) % 4
            Sb[j - 1] = (T[core, n].astype(F32) + Ra[n].astype(F32)).astype(BF)
            rs_copy(k, 1, j).start()

    def stage2(k):
        a1, a2 = at[order(k)[0]], at[order(k)[1]]
        T, Ra, Rb, Sc = s[f"T{k}"], s[f"Ra{k}"], s[f"Rb{k}"], s[f"Sc{k}"]
        for j in (1, 2, 3):
            rs_copy(k, 1, j).wait_recv()
        for j in (1, 2, 3, 4):
            n = (a2 + j) % 4
            total = T[core, a1, n].astype(F32) + Ra[a1, n].astype(F32)
            for i in range(3):
                total = total + Rb[i, n].astype(F32)
            Sc[j - 1] = total
            if j < 4:
                rs_copy(k, 2, j).start()

    def stage3(k):
        a3 = at[order(k)[2]]
        Sc, Rc, Sd = s[f"Sc{k}"], s[f"Rc{k}"], s[f"Sd{k}"]
        for j in (1, 2, 3):
            rs_copy(k, 2, j).wait_recv()
        for j in (1, 2, 3, 4):
            n = (a3 + j) % 4
            Sd[j - 1] = Sc[3, n] + Rc[0, n] + Rc[1, n] + Rc[2, n]
            if j < 4:
                rs_copy(k, 3, j).start()

    def finish(k):
        name, c0, w, _ = CHUNKS[k]
        Sd, Rd = s[f"Sd{k}"], s[f"Rd{k}"]
        for j in (1, 2, 3):
            rs_copy(k, 3, j).wait_recv()
        total = Sd[3] + Rd[0] + Rd[1] + Rd[2]
        out = gdn_out if name == "down" else gin_out
        out[:, c0 : c0 + w] = total[0:15, 0:w]
        return total

    hall = s["hall"]
    h1, h2, h3 = (at[a] for a in order(0))

    def ag_copy(n, j=1):
        part = [hall.at[core, h1, h2, h3], hall.at[core, h1, h2], hall.at[core, h1], hall.at[core]][n]
        dev = partner("c", 1) if n == 3 else partner(order(0)[2 - n], j)
        m = 9 if n == 3 else 3 * n + j - 1
        return remote(part, part, s["ag_ss"].at[m], s["ag_rs"].at[m], dev)

    def ag_start(n):
        for j in (1,) if n == 3 else (1, 2, 3):
            ag_copy(n, j).start()

    def ag_wait(n):
        for j in (1,) if n == 3 else (1, 2, 3):
            ag_copy(n, j).wait_recv()

    def ar_copy(n, j=1):
        axis = "cxyz"[n]
        buf = s["ar" + axis]
        m = 0 if n == 0 else 3 * n - 3 + j
        part = buf.at[at[axis]]
        return remote(part, part, s["ar_ss"].at[m], s["ar_rs"].at[m], partner(axis, j))

    def ar_start(n, value):
        axis = "cxyz"[n]
        s["ar" + axis][at[axis]] = value
        for j in (1,) if n == 0 else (1, 2, 3):
            ar_copy(n, j).start()

    def ar_sum(n):
        buf = s["ar" + "cxyz"[n]]
        for j in (1,) if n == 0 else (1, 2, 3):
            ar_copy(n, j).wait_recv()
        total = buf[0]
        for i in range(1, 2 if n == 0 else 4):
            total = total + buf[i]
        return total

    def grad_hidden(ci):
        rows = pl.ds(pl.multiple_of(ci * ROWS, ROWS), ROWS)
        for k in range(7):
            g_copy(ci, k).wait_recv()
        s["ghid"][rows, :] = dot(
            s["grecv"][ci].reshape(ROWS, OUTC), s["whd"][...], 1, 1
        ).astype(BF)

    def backward(ci):
        i = (ci + 1) % LATD
        rows = pl.ds(pl.multiple_of(ci * ROWS, ROWS), ROWS)
        ghid = s["ghid"][rows, :]
        for f in range(4):
            cols = slice(f * 512, f * 512 + 512)
            gact = dot(ghid, s["wdn"][cols, :], 1, 1)
            s["gpre"][rows, cols] = (s["slope"][rows, cols] * gact).astype(BF)
        s["cbuf"][...] = dot(s["gpre"][rows, :], s["win"][...], 1, 0)
        gain_acc = jnp.zeros((8, D), F32)
        for q in range(ROWS // 32):
            here = slice(q * 32, q * 32 + 32)
            gn = s["cbuf"][here, :]
            normal = s["normal"][ci, here, :]
            inv = s["istd"][ci, here, 0:1]
            gain_acc = gain_acc + jnp.sum((gn * normal).reshape(4, 8, D), axis=0)
            g = gn * gain
            s["cbuf"][here, :] = (
                g
                - jnp.mean(g, axis=-1, keepdims=True)
                - normal * jnp.mean(g * normal, axis=-1, keepdims=True)
            ) * inv
        s["cacc"][9] = s["cacc"][9] + gain_acc
        for lt in range(D // 128):
            lanes = slice(lt * 128, lt * 128 + 128)
            acc = [s["cacc"][n, :, lanes] for n in range(9)]
            for m in range(MEM):
                g1 = s["cbuf"][m * LON : (m + 1) * LON, lanes]
                moved = [pltpu.roll(g1, LON - 1, 0), g1, pltpu.roll(g1, 1, 0)]
                for a in range(3):
                    cells = mixed[i + a, m, :, lanes].astype(F32)
                    for b in range(3):
                        acc[3 * a + b] = acc[3 * a + b] + jnp.sum(
                            (cells * moved[b]).reshape(16, 8, 128), axis=0
                        )
            for n in range(9):
                s["cacc"][n, :, lanes] = acc[n]

    @pl.loop(0, LATD)
    def _(ci):
        @pl.when(ci == 1)
        def _():
            score(LATD - 1)

        @pl.when(ci < 2)
        def _():
            grad_hidden(ci)

        @pl.when(ci == 2)
        def _():
            grad_hidden(2)
            grad_hidden(3)
            head_product(0)
            product(0, s["activ"], s["ghid"])
            rs_copy(0, 0).start()
            product(1, s["activ"], s["ghid"])
            rs_copy(1, 0).start()
            stage1(0)
            product(2, s["activ"], s["ghid"])
            rs_copy(2, 0).start()
            stage1(1)

        backward(ci)

        @pl.when(ci == 2)
        def _():
            stage1(2)

    ar_start(0, jnp.sum(s["cacc"][...], axis=1))
    stage2(0)
    product(3, s["gpre"], s["normed"])
    rs_copy(3, 0).start()
    stage2(1)
    ar_start(1, ar_sum(0))
    product(4, s["gpre"], s["normed"])
    rs_copy(4, 0).start()
    stage1(3)
    stage2(2)
    stage3(0)
    product(5, s["gpre"], s["normed"])
    rs_copy(5, 0).start()
    stage1(4)
    ar_start(2, ar_sum(1))
    stage3(1)
    stage1(5)
    stage3(2)
    total = finish(0)
    hall[core, h1, h2, h3] = total[:, 128:256]
    ag_start(0)
    finish(1)
    finish(2)
    ar_start(3, ar_sum(2))
    ag_wait(0)
    ag_start(1)
    stage2(3)
    stage2(4)
    stage2(5)
    ag_wait(1)
    ag_start(2)
    sums = ar_sum(3)
    conv_out[...] = sums[0:9]
    gain_out[...] = sums[9:10]
    stage3(3)
    stage3(4)
    stage3(5)
    ag_wait(2)
    ag_start(3)
    finish(3)
    finish(4)
    finish(5)
    ag_wait(3)
    for t in range(HEAD_TILES):
        i1, i2, i3 = spot(0, t // 64, (t // 16) % 4, (t // 8) % 2, (t // 2) % 4)
        rt, ct = t // 3, t % 3
        n = min(128, OUTC - ct * 128)
        head_out[rt * 16 : rt * 16 + 16, ct * 128 : ct * 128 + n] = hall[t % 2, i1, i2, i3, :, 0:n]

    @pl.loop(0, LATD)
    def _(ci):
        for k in range(7):
            y_copy(ci, k).wait_send()
            g_copy(ci, k).wait_send()

    for k in range(6):
        rs_copy(k, 0).wait_send()
        for stage in (1, 2, 3):
            for j in (1, 2, 3):
                rs_copy(k, stage, j).wait_send()
    for n in range(4):
        for j in (1,) if n == 3 else (1, 2, 3):
            ag_copy(n, j).wait_send()
        for j in (1,) if n == 0 else (1, 2, 3):
            ar_copy(n, j).wait_send()


def body(
    latent_state, member_noise, conv_weight, norm_gain, weight_in, weight_down, weight_head, target_field
):
    vmem = pl.BlockSpec(memory_space=pltpu.VMEM)
    hbm = pl.BlockSpec(memory_space=pl.ANY)
    gin, gdn, head, gain, conv = pl.pallas_call(
        kernel,
        name="ensemble_block",
        out_shape=(
            jax.ShapeDtypeStruct((15, D), F32),
            jax.ShapeDtypeStruct((15, D), F32),
            jax.ShapeDtypeStruct((D, OUTC), F32),
            jax.ShapeDtypeStruct((1, D), F32),
            jax.ShapeDtypeStruct((9, D), F32),
        ),
        in_specs=[hbm, hbm, vmem, vmem, hbm, hbm, hbm, hbm],
        out_specs=(vmem,) * 5,
        scratch_shapes=list(scratch().values()),
        compiler_params=pltpu.CompilerParams(
            collective_id=0, has_side_effects=True, vmem_limit_bytes=62 * 2**20
        ),
        cost_estimate=pl.CostEstimate(
            flops=17_000_000_000, bytes_accessed=9_000_000, transcendentals=2_100_000
        ),
    )(
        latent_state, member_noise, conv_weight, norm_gain.reshape(1, D), weight_in, weight_down,
        weight_head, target_field,
    )
    return gin, gdn, head, gain.reshape(D), conv


def solution(mesh):
    return jax.shard_map(
        body,
        mesh=mesh,
        in_specs=(
            P("space", None, None),
            P("member", "space", None, None),
            P(),
            P(),
            P(),
            P(),
            P(),
            P("space", None, None),
        ),
        out_specs=(P(("member", "space"), None), P(("member", "space"), None), P(), P(), P()),
        check_vma=False,
    )
```

profile of v0, /device:TPU:1, one launch (start us, length us, event | category | flops | bytes accessed | tf_op | source)
XLA Modules:
  0.0 100.5 jit_solution(4747063422136287302)
XLA Ops:
  0.6 1.3 %reshape.16.gain_ref = f32[1,640]{1,0:T(1,128)} reshape(f32[640]{0:T(1024)} %param.11) | data formatting | bytes 5120 | tf_op jit(solution)/shard_map/reshape | solution.py:610
  1.9 2.0 %copy.13.whd_hbm = bf16[640,320]{1,0:T(8,128)(2,1)} copy(bf16[640,320]{0,1:T(8,128)(2,1)} %param.14) | data formatting | bytes 819200 | tf_op args[6]
  3.9 2.2 %copy.14.tgt_hbm = f32[4,128,320]{2,1,0:T(8,128)} copy(f32[4,128,320]{1,2,0:T(8,128)} %param.15) | data formatting | bytes 1310720 | tf_op args[7]
  6.1 86.5 %ensemble_block.1 = (f32[15,640]{1,0:T(8,128)}, f32[15,640]{1,0:T(8,128)}, f32[640,320]{1,0:T(8,128)}, f32[1,640]{1,0:T(1,128)}, f32[9,640]{1,0:T(8,128)}) custom-call(bf16[4,128,640]{2,1,0:T(8,128)(2,1)} %lat_hbm.1, bf16[2,4,128,640]{3,2,1,0:T(8,128)(2,1)} %noise_hbm.1, f32[9,640]{1,0:T(8,128)} %cw_ref.1, f32[1,640]{1,0:T(1,128)} %reshape.16.gain_ref, ...), custom_call_target="tpu_custom_call" | custom-call | flops 16999999488 | bytes 9000000 | tf_op jit(solution)/shard_map/ensemble_block/pallas_call | solution.py:590
  92.6 1.3 %reduce = f32[640]{0:T(1024)} reduce(f32[1,640]{1,0:T(1,128)} %get-tuple-element.13, f32[]{:T(128)} %constant.3), dimensions={0}, to_apply=%get-tuple-element.13.reduce_sub_computation | reduce | bytes 5124 | tf_op jit(solution)/shard_map/ensemble_block/pallas_call | solution.py:590
  93.9 2.4 %copy.15 = f32[640,320]{0,1:T(8,128)} copy(f32[640,320]{1,0:T(8,128)} %get-tuple-element.17) | data formatting | bytes 1638400
  96.3 1.4 %copy.19 = f32[15,640]{1,0:T(8,128)} copy(f32[15,640]{1,0:T(8,128)} %get-tuple-element.25) | data formatting | bytes 76800
  97.7 1.4 %copy.20 = f32[15,640]{1,0:T(8,128)} copy(f32[15,640]{1,0:T(8,128)} %get-tuple-element.26) | data formatting | bytes 76800
  99.1 1.4 %copy.21 = f32[9,640]{1,0:T(8,128)} copy(f32[9,640]{1,0:T(8,128)} %get-tuple-element.29) | data formatting | bytes 46080
where the time goes:
time: 101 us; the launch traced here: 100 us
  Pallas kernels  86.5 us (86%)
  local copies, waits for them, and re-layouts  12.1 us (12%)
  other arithmetic  1.27 us (1%)
    pallas_call x1, Pallas kernels, body(): pl.pallas_call(kernel, name='ensemble_block', out_shape=(jax.ShapeDtypeSt...  86.5 us
    unnamed x6, local copies, waits for them, and re-layouts  10.8 us

commit v1 on v0

--- a/solution.py
+++ b/solution.py
@@ -26,15 +26,15 @@
 GC = math.sqrt(2.0 / math.pi)
 GROUP = [(dz, dy) for dz in range(4) for dy in range(2)][1:]
 CHUNKS = [
-    ("down", 512, 128, "zxy"),
+    ("head", 0, 128, "zxy"),
     ("down", 0, 256, "xyz"),
     ("down", 256, 256, "yzx"),
+    ("down", 512, 128, "zxy"),
     ("in", 0, 256, "xyz"),
     ("in", 256, 256, "yzx"),
     ("in", 512, 128, "zxy"),
 ]
-WIDTH = [256, 256, 256, 256, 256, 128]
-HEAD_TILES = 120
+HEAD_TILES = 100
 
 
 def dot(a, b, ca, cb):
@@ -43,18 +43,15 @@
 
 def scratch():
     out = {
-        "noise": pltpu.VMEM((LATD, MEM, LON, D), BF),
-        "latent": pltpu.VMEM((LATD, LON, D), BF),
-        "wraw": pltpu.VMEM((FFR, D), BF),
         "win": pltpu.VMEM((FF, D), BF),
         "wdn": pltpu.VMEM((FF, D), BF),
-        "whd": pltpu.VMEM((D, OUTC), BF),
-        "tgt": pltpu.VMEM((LATD, 16, OUTC), F32),
+        "whd": pltpu.VMEM((OUTC, D), BF),
+        "tgt": pltpu.VMEM((LATD, LON, OUTC), F32),
         "mixed": pltpu.VMEM((LATD + 2, MEM, LON, D), BF),
-        "cbuf": pltpu.VMEM((ROWS, D), F32),
-        "normal": pltpu.VMEM((LATD, ROWS, D), F32),
-        "istd": pltpu.VMEM((LATD, ROWS, 128), F32),
-        "normed": pltpu.VMEM((LATD * ROWS, D), BF),
+        "cbuf": pltpu.VMEM((2 * ROWS, D), F32),
+        "normal": pltpu.VMEM((LATD + 1, ROWS, D), F32),
+        "istd": pltpu.VMEM((LATD + 1, ROWS, 128), F32),
+        "normed": pltpu.VMEM(((LATD + 1) * ROWS, D), BF),
         "slope": pltpu.VMEM((LATD * ROWS, FF), F32),
         "activ": pltpu.VMEM((LATD * ROWS, FF), BF),
         "gpre": pltpu.VMEM((LATD * ROWS, FF), BF),
@@ -65,32 +62,43 @@
         "gsend": pltpu.VMEM((LATD, MEMBERS, 16, OUTC), BF),
         "grecv": pltpu.VMEM((LATD, MEM, LON, OUTC), BF),
         "cacc": pltpu.VMEM((10, 8, D), F32),
-        "hall": pltpu.VMEM((2, 4, 4, 4, 16, 128), F32),
+        "hall": pltpu.VMEM((2, 4, 4, 4, 16, 128), BF),
         "arc": pltpu.VMEM((2, 10, D), F32),
         "arx": pltpu.VMEM((4, 10, D), F32),
         "ary": pltpu.VMEM((4, 10, D), F32),
         "arz": pltpu.VMEM((4, 10, D), F32),
-        "l_sem": pltpu.SemaphoreType.DMA((LATD + 5,)),
+        "cw": pltpu.VMEM((9, D), F32),
+        "gain": pltpu.VMEM((D,), F32),
+        "o_gin": pltpu.VMEM((15, D), F32),
+        "o_gdn": pltpu.VMEM((15, D), F32),
+        "o_head": pltpu.VMEM((OUTC, D), F32),
+        "o_gain": pltpu.VMEM((D,), F32),
+        "o_conv": pltpu.VMEM((9, D), F32),
+        "o_sem": pltpu.SemaphoreType.DMA((5,)),
+        "l_sem": pltpu.SemaphoreType.DMA((LATD + 3,)),
+        "i_sem": pltpu.SemaphoreType.DMA((LATD, MEM + 1)),
+        "w_sem": pltpu.SemaphoreType.DMA((2, 8)),
         "h_ss": pltpu.SemaphoreType.DMA((2,)),
         "h_rs": pltpu.SemaphoreType.DMA((2,)),
         "y_ss": pltpu.SemaphoreType.DMA((LATD, 7)),
         "y_rs": pltpu.SemaphoreType.DMA((LATD, 7)),
         "g_ss": pltpu.SemaphoreType.DMA((LATD, 7)),
         "g_rs": pltpu.SemaphoreType.DMA((LATD, 7)),
-        "r_ss": pltpu.SemaphoreType.DMA((6, 10)),
-        "r_rs": pltpu.SemaphoreType.DMA((6, 10)),
+        "r_ss": pltpu.SemaphoreType.DMA((7, 10)),
+        "r_rs": pltpu.SemaphoreType.DMA((7, 10)),
         "ag_ss": pltpu.SemaphoreType.DMA((10,)),
         "ag_rs": pltpu.SemaphoreType.DMA((10,)),
         "ar_ss": pltpu.SemaphoreType.DMA((10,)),
         "ar_rs": pltpu.SemaphoreType.DMA((10,)),
     }
-    for k, w in enumerate(WIDTH):
+    for k, (_, _, w, _) in enumerate(CHUNKS):
         out[f"T{k}"] = pltpu.VMEM((2, 4, 4, 4, 16, w), BF)
         out[f"Ra{k}"] = pltpu.VMEM((4, 4, 4, 16, w), BF)
         out[f"Sb{k}"] = pltpu.VMEM((3, 4, 4, 16, w), BF)
         out[f"Rb{k}"] = pltpu.VMEM((3, 4, 4, 16, w), BF)
-        out[f"Sc{k}"] = pltpu.VMEM((4, 4, 16, w), F32)
-        out[f"Rc{k}"] = pltpu.VMEM((3, 4, 16, w), F32)
+        out[f"Sc{k}"] = pltpu.VMEM((3, 4, 16, w), BF)
+        out[f"Oc{k}"] = pltpu.VMEM((4, 16, w), F32)
+        out[f"Rc{k}"] = pltpu.VMEM((3, 4, 16, w), BF)
         out[f"Sd{k}"] = pltpu.VMEM((4, 16, w), F32)
         out[f"Rd{k}"] = pltpu.VMEM((3, 16, w), F32)
     return out
@@ -100,8 +108,8 @@
 
 
 def kernel(
-    lat_hbm, noise_hbm, cw_ref, gain_ref, win_hbm, wdn_hbm, whd_hbm, tgt_hbm,
-    gin_out, gdn_out, head_out, gain_out, conv_out, *refs,
+    lat_hbm, noise_hbm, cw_hbm, gain_hbm, win_hbm, wdn_hbm, whd_hbm, tgt_hbm,
+    gin_hbm, gdn_hbm, head_hbm, ggain_hbm, gconv_hbm, *refs,
 ):
     s = dict(zip(NAMES, refs))
     member = lax.axis_index("member")
@@ -139,35 +147,77 @@
         pl.semaphore_signal(barrier, inc=1, device_id=dev, device_id_type=MESH)
 
     lsem = s["l_sem"]
-    lat_cp = pltpu.make_async_copy(lat_hbm, s["latent"], lsem.at[LATD])
-    noise_cp = [
-        pltpu.make_async_copy(noise_hbm.at[:, i], s["noise"].at[i], lsem.at[i]) for i in range(LATD)
+
+    def cells_raw(i, m):
+        n = (i * MEM + m) * LON
+        return s["hidden"].at[n : n + LON]
+
+    def latent_raw(i):
+        return s["ghid"].at[i * LON : i * LON + LON]
+
+    cells_cp = [
+        [
+            pltpu.make_async_copy(noise_hbm.at[m, i], cells_raw(i, m), s["i_sem"].at[i, m])
+            for m in range(MEM)
+        ]
+        + [pltpu.make_async_copy(lat_hbm.at[i], latent_raw(i), s["i_sem"].at[i, MEM])]
+        for i in range(LATD)
     ]
-    win_cp = pltpu.make_async_copy(win_hbm, s["wraw"], lsem.at[LATD + 1])
-    wdn_cp = pltpu.make_async_copy(wdn_hbm, s["wraw"], lsem.at[LATD + 2])
-    whd_cp = pltpu.make_async_copy(whd_hbm, s["whd"], lsem.at[LATD + 3])
+
+    def raw(name, b):
+        r, c = (b % 4) * 240, (b // 4) * D
+        return s[name].at[r : r + 240, c : c + D]
+
+    win_cp = [
+        pltpu.make_async_copy(win_hbm.at[240 * b : 240 * b + 240], raw("activ", b), s["w_sem"].at[0, b])
+        for b in range(8)
+    ]
+    wdn_cp = [
+        pltpu.make_async_copy(wdn_hbm.at[240 * b : 240 * b + 240], raw("gpre", b), s["w_sem"].at[1, b])
+        for b in range(8)
+    ]
+    whd_cp = pltpu.make_async_copy(whd_hbm, s["whd"], lsem.at[LATD])
+
+    def traw(i):
+        return s["slope"].at[0:OUTC, LON * i : LON * i + LON]
+
+    tgt_cp = [
+        pltpu.make_async_copy(tgt_hbm.at[i], traw(i), lsem.at[i]) for i in range(LATD)
+    ]
+    cw_cp = pltpu.make_async_copy(cw_hbm, s["cw"], lsem.at[LATD + 1])
+    gain_cp = pltpu.make_async_copy(gain_hbm, s["gain"], lsem.at[LATD + 2])
+    out_cp = [
+        pltpu.make_async_copy(s[n], dst, s["o_sem"].at[k])
+        for k, (n, dst) in enumerate(
+            (
+                ("o_gin", gin_hbm),
+                ("o_gdn", gdn_hbm),
+                ("o_head", head_hbm),
+                ("o_gain", ggain_hbm),
+                ("o_conv", gconv_hbm),
+            )
+        )
+    ]
     mine16 = pl.ds(pl.multiple_of(member * 16, 16), 16)
-    tgt_cp = pltpu.make_async_copy(tgt_hbm.at[:, mine16], s["tgt"], lsem.at[LATD + 4])
-    lat_cp.start()
     for i in (0, 3, 1, 2):
-        noise_cp[i].start()
-    win_cp.start()
-    whd_cp.start()
-    tgt_cp.start()
+        for cp in cells_cp[i]:
+            cp.start()
+    for cp in (cw_cp, gain_cp, *win_cp, *wdn_cp, whd_cp, *tgt_cp):
+        cp.start()
 
     mixed = s["mixed"]
 
     def mix(i):
-        noise_cp[i].wait()
-        base = s["latent"][i].astype(F32)
+        for cp in cells_cp[i]:
+            cp.wait()
+        base = latent_raw(i)[...].astype(F32)
         for m in range(MEM):
-            mixed[i + 1, m] = (base + s["noise"][i, m].astype(F32)).astype(BF)
+            mixed[i + 1, m] = (base + cells_raw(i, m)[...].astype(F32)).astype(BF)
 
     halo_cp = [
         remote(mixed.at[1], mixed.at[5], s["h_ss"].at[0], s["h_rs"].at[0], halo(-1)),
         remote(mixed.at[4], mixed.at[0], s["h_ss"].at[1], s["h_rs"].at[1], halo(1)),
     ]
-    lat_cp.wait()
     mix(0)
     mix(3)
     pl.semaphore_wait(barrier, len(friends))
@@ -182,20 +232,12 @@
         (row_at % 16 < 15) & (col_at == (row_at // 16) * 15 + row_at % 16), 1.0, 0.0
     ).astype(BF)
 
-    def pad_rows(dst):
+    def pad_rows(dst, name):
         for b in range(8):
+            r, c = (b % 4) * 240, (b // 4) * D
             dst[256 * b : 256 * b + 256, :] = dot(
-                spread, s["wraw"][240 * b : 240 * b + 240, :], 1, 0
+                spread, s[name][r : r + 240, c : c + D], 1, 0
             ).astype(BF)
-
-    win_cp.wait()
-    pad_rows(s["win"])
-    wdn_cp.start()
-    s["cacc"][...] = jnp.zeros((10, 8, D), F32)
-    wdn_cp.wait()
-    pad_rows(s["wdn"])
-    whd_cp.wait()
-    tgt_cp.wait()
 
     def y_copy(ci, k):
         dz, dy = GROUP[k]
@@ -215,12 +257,10 @@
             s["g_ss"].at[ci, k], s["g_rs"].at[ci, k], (to, space),
         )
 
-    gain = gain_ref[...]
-
-    def forward(ci):
+
+    def conv_norm(ci):
         i = (ci + 1) % LATD
         r0 = pl.multiple_of(ci * ROWS, ROWS)
-        rows = pl.ds(r0, ROWS)
         for m in range(MEM):
             for lt in range(D // 128):
                 lanes = slice(lt * 128, lt * 128 + 128)
@@ -228,7 +268,7 @@
                 for a in range(3):
                     cells = mixed[i + a, m, :, lanes].astype(F32)
                     for b in range(3):
-                        term = cw_ref[3 * a + b : 3 * a + b + 1, lanes] * cells
+                        term = s["cw"][3 * a + b : 3 * a + b + 1, lanes] * cells
                         part[b] = term if a == 0 else part[b] + term
                 s["cbuf"][m * LON : (m + 1) * LON, lanes] = (
                     part[1] + pltpu.roll(part[0], 1, 0) + pltpu.roll(part[2], LON - 1, 0)
@@ -242,6 +282,10 @@
             s["normal"][ci, here, :] = normal
             s["istd"][ci, here, :] = jnp.broadcast_to(inv, (32, 128))
             s["normed"][pl.ds(pl.multiple_of(r0 + q * 32, 32), 32), :] = (normal * gain).astype(BF)
+
+    def mixer(ci):
+        i = (ci + 1) % LATD
+        rows = pl.ds(pl.multiple_of(ci * ROWS, ROWS), ROWS)
         normed = s["normed"][rows, :]
         for f in range(4):
             cols = slice(f * 512, f * 512 + 512)
@@ -256,11 +300,9 @@
         base = mixed[i + 1].reshape(ROWS, D).astype(F32)
         hidden = (base + down).astype(BF)
         s["hidden"][rows, :] = hidden
-        pred = dot(hidden, s["whd"][...], 1, 0)
+        pred = dot(hidden, s["whd"][...], 1, 1)
         s["ysend"][ci] = pred.astype(BF).reshape(MEM, LON, OUTC)
         s["yrecv"][ci, pl.ds(member * 2, 2)] = s["ysend"][ci, :, mine16]
-        for k in range(7):
-            y_copy(ci, k).start()
 
     def score(ci):
         i = (ci + 1) % LATD
@@ -278,7 +320,7 @@
         w_sum = jnp.sum(w.astype(F32), axis=1, keepdims=True)
         pulled = dot(w, yb, 1, 0)
         yf = yb.astype(F32)
-        err = (yf.reshape(16, 16, OUTC) - s["tgt"][i][None]).reshape(256, OUTC)
+        err = (yf.reshape(16, 16, OUTC) - s["tgt"][i, mine16, :][None]).reshape(256, OUTC)
         far = lax.rsqrt(jnp.sum(err * err, axis=-1, keepdims=True) + 1.0)
         grad = err * (far * (SCALE / MEMBERS)) - (yf * w_sum - pulled) * (
             SCALE / (MEMBERS * (MEMBERS - 1))
@@ -288,9 +330,21 @@
         for k in range(7):
             g_copy(ci, k).start()
 
+    for cp in (cw_cp, gain_cp):
+        cp.wait()
+    s["cacc"][...] = jnp.zeros((10, 8, D), F32)
+    gain = s["gain"][...].reshape(1, D)
+    conv_norm(0)
+    for cp in (*win_cp, *wdn_cp, whd_cp, *tgt_cp):
+        cp.wait()
+    pad_rows(s["win"], "activ")
+    pad_rows(s["wdn"], "gpre")
+    for i in range(LATD):
+        s["tgt"][i] = traw(i)[...].T
+
     @pl.loop(0, LATD)
     def _(ci):
-        @pl.when(ci == 2)
+        @pl.when(ci == 1)
         def _():
             for cp in halo_cp:
                 cp.wait()
@@ -303,7 +357,10 @@
             def _():
                 mixed[5] = jnp.zeros((MEM, LON, D), BF)
 
-        forward(ci)
+        mixer(ci)
+        conv_norm(ci + 1)
+        for k in range(7):
+            y_copy(ci, k).start()
 
         @pl.when(ci > 0)
         def _():
@@ -334,7 +391,10 @@
         @pl.loop(0, 2)
         def _(o_ylo):
             half = dot(
-                left[:, pl.ds(pl.multiple_of(o_ylo * 1024, 1024), 1024)], right[:, c0 : c0 + w], 0, 0
+                left[:, pl.ds(pl.multiple_of(o_ylo * 1024, 1024), 1024)],
+                right[0 : LATD * ROWS, c0 : c0 + w],
+                0,
+                0,
             ).astype(BF)
             for g in range(64):
                 o_z, o_yhi, o_x, o_c = g // 16, (g // 8) % 2, (g // 2) % 4, g % 2
@@ -343,18 +403,14 @@
 
     def head_product(k):
         T = s[f"T{k}"]
-        grad = dot(s["hidden"][...], s["grecv"][...].reshape(LATD * ROWS, OUTC), 0, 0).astype(BF)
+        grad = dot(s["grecv"][...].reshape(LATD * ROWS, OUTC), s["hidden"][...], 0, 0).astype(BF)
         for t in range(128):
             i1, i2, i3 = spot(k, t // 64, (t // 16) % 4, (t // 8) % 2, (t // 2) % 4)
-            at_ = (t % 2, i1, i2, i3)
-            if t >= HEAD_TILES:
-                T[(*at_, slice(None), slice(128, 256))] = jnp.zeros((16, 128), BF)
-                continue
-            rt, ct = t // 3, t % 3
-            tile = grad[rt * 16 : rt * 16 + 16, ct * 128 : min(OUTC, ct * 128 + 128)]
-            if ct == 2:
-                T[(*at_, slice(None), slice(192, 256))] = jnp.zeros((16, 64), BF)
-            T[(*at_, slice(None), slice(128, 128 + tile.shape[1]))] = tile
+            rt, ct = t // 5, t % 5
+            if t < HEAD_TILES:
+                T[t % 2, i1, i2, i3] = grad[rt * 16 : rt * 16 + 16, ct * 128 : ct * 128 + 128]
+            else:
+                T[t % 2, i1, i2, i3] = jnp.zeros((16, 128), BF)
 
     def stage1(k):
         a1 = at[order(k)[0]]
@@ -375,18 +431,23 @@
             total = T[core, a1, n].astype(F32) + Ra[a1, n].astype(F32)
             for i in range(3):
                 total = total + Rb[i, n].astype(F32)
-            Sc[j - 1] = total
             if j < 4:
+                Sc[j - 1] = total.astype(BF)
                 rs_copy(k, 2, j).start()
+            else:
+                s[f"Oc{k}"][...] = total
 
     def stage3(k):
         a3 = at[order(k)[2]]
-        Sc, Rc, Sd = s[f"Sc{k}"], s[f"Rc{k}"], s[f"Sd{k}"]
+        Oc, Rc, Sd = s[f"Oc{k}"], s[f"Rc{k}"], s[f"Sd{k}"]
         for j in (1, 2, 3):
             rs_copy(k, 2, j).wait_recv()
         for j in (1, 2, 3, 4):
             n = (a3 + j) % 4
-            Sd[j - 1] = Sc[3, n] + Rc[0, n] + Rc[1, n] + Rc[2, n]
+            total = Oc[n]
+            for i in range(3):
+                total = total + Rc[i, n].astype(F32)
+            Sd[j - 1] = total
             if j < 4:
                 rs_copy(k, 3, j).start()
 
@@ -396,9 +457,11 @@
         for j in (1, 2, 3):
             rs_copy(k, 3, j).wait_recv()
         total = Sd[3] + Rd[0] + Rd[1] + Rd[2]
-        out = gdn_out if name == "down" else gin_out
-        out[:, c0 : c0 + w] = total[0:15, 0:w]
-        return total
+        if name == "head":
+            hall[core, h1, h2, h3] = total.astype(BF)
+        else:
+            out = s["o_gdn"] if name == "down" else s["o_gin"]
+            out[:, c0 : c0 + w] = total[0:15, :]
 
     hall = s["hall"]
     h1, h2, h3 = (at[a] for a in order(0))
@@ -439,32 +502,39 @@
             total = total + buf[i]
         return total
 
-    def grad_hidden(ci):
-        rows = pl.ds(pl.multiple_of(ci * ROWS, ROWS), ROWS)
-        for k in range(7):
-            g_copy(ci, k).wait_recv()
+    def grad_hidden(ci, n):
+        rows = pl.ds(pl.multiple_of(ci * ROWS, ROWS), n * ROWS)
+        for i in range(n):
+            for k in range(7):
+                g_copy(ci + i, k).wait_recv()
         s["ghid"][rows, :] = dot(
-            s["grecv"][ci].reshape(ROWS, OUTC), s["whd"][...], 1, 1
+            s["grecv"][pl.ds(ci, n)].reshape(n * ROWS, OUTC), s["whd"][...], 1, 0
         ).astype(BF)
 
-    def backward(ci):
-        i = (ci + 1) % LATD
-        rows = pl.ds(pl.multiple_of(ci * ROWS, ROWS), ROWS)
+    def grad_act(ci, n):
+        rows = pl.ds(pl.multiple_of(ci * ROWS, ROWS), n * ROWS)
         ghid = s["ghid"][rows, :]
         for f in range(4):
             cols = slice(f * 512, f * 512 + 512)
             gact = dot(ghid, s["wdn"][cols, :], 1, 1)
             s["gpre"][rows, cols] = (s["slope"][rows, cols] * gact).astype(BF)
-        s["cbuf"][...] = dot(s["gpre"][rows, :], s["win"][...], 1, 0)
+
+    def grad_normed(ci, n):
+        rows = pl.ds(pl.multiple_of(ci * ROWS, ROWS), n * ROWS)
+        s["cbuf"][0 : n * ROWS, :] = dot(s["gpre"][rows, :], s["win"][...], 1, 0)
+
+    def conv_back(ci, r0):
+        i = (ci + 1) % LATD
         gain_acc = jnp.zeros((8, D), F32)
         for q in range(ROWS // 32):
             here = slice(q * 32, q * 32 + 32)
-            gn = s["cbuf"][here, :]
+            there = slice(r0 + q * 32, r0 + q * 32 + 32)
+            gn = s["cbuf"][there, :]
             normal = s["normal"][ci, here, :]
             inv = s["istd"][ci, here, 0:1]
             gain_acc = gain_acc + jnp.sum((gn * normal).reshape(4, 8, D), axis=0)
             g = gn * gain
-            s["cbuf"][here, :] = (
+            s["cbuf"][there, :] = (
                 g
                 - jnp.mean(g, axis=-1, keepdims=True)
                 - normal * jnp.mean(g * normal, axis=-1, keepdims=True)
@@ -474,7 +544,7 @@
             lanes = slice(lt * 128, lt * 128 + 128)
             acc = [s["cacc"][n, :, lanes] for n in range(9)]
             for m in range(MEM):
-                g1 = s["cbuf"][m * LON : (m + 1) * LON, lanes]
+                g1 = s["cbuf"][r0 + m * LON : r0 + (m + 1) * LON, lanes]
                 moved = [pltpu.roll(g1, LON - 1, 0), g1, pltpu.roll(g1, 1, 0)]
                 for a in range(3):
                     cells = mixed[i + a, m, :, lanes].astype(F32)
@@ -485,84 +555,61 @@
             for n in range(9):
                 s["cacc"][n, :, lanes] = acc[n]
 
-    @pl.loop(0, LATD)
+    @pl.loop(0, 3)
     def _(ci):
-        @pl.when(ci == 1)
+        @pl.when(ci == 2)
         def _():
             score(LATD - 1)
 
-        @pl.when(ci < 2)
-        def _():
-            grad_hidden(ci)
-
-        @pl.when(ci == 2)
-        def _():
-            grad_hidden(2)
-            grad_hidden(3)
-            head_product(0)
-            product(0, s["activ"], s["ghid"])
-            rs_copy(0, 0).start()
-            product(1, s["activ"], s["ghid"])
-            rs_copy(1, 0).start()
-            stage1(0)
-            product(2, s["activ"], s["ghid"])
-            rs_copy(2, 0).start()
-            stage1(1)
-
-        backward(ci)
-
-        @pl.when(ci == 2)
-        def _():
-            stage1(2)
-
+        grad_hidden(ci, 1)
+        grad_act(ci, 1)
+        grad_normed(ci, 1)
+        conv_back(ci, 0)
+
+    def send0(k):
+        rs_copy(k, 0).start()
+
+    def sent(*stages):
+        for k in range(7):
+            for stage in stages:
+                for j in (1,) if stage == 0 else (1, 2, 3):
+                    rs_copy(k, stage, j).wait_send()
+
+    activ, ghid, gpre, normed = s["activ"], s["ghid"], s["gpre"], s["normed"]
+    grad_hidden(3, 1)
+    head_product(0)
+    send0(0)
+    product(1, activ, ghid)
+    send0(1)
+    stage1(0)
+    product(2, activ, ghid)
+    send0(2)
+    stage1(1)
+    product(3, activ, ghid)
+    send0(3)
+    stage1(2)
+    grad_act(3, 1)
+    stage1(3)
+    stage2(0)
+    product(4, gpre, normed)
+    send0(4)
+    product(5, gpre, normed)
+    send0(5)
+    stage1(4)
+    stage3(0)
+    grad_normed(3, 1)
+    stage1(5)
+    stage2(1)
+    conv_back(3, 0)
     ar_start(0, jnp.sum(s["cacc"][...], axis=1))
-    stage2(0)
-    product(3, s["gpre"], s["normed"])
-    rs_copy(3, 0).start()
-    stage2(1)
+    product(6, gpre, normed)
+    send0(6)
     ar_start(1, ar_sum(0))
-    product(4, s["gpre"], s["normed"])
-    rs_copy(4, 0).start()
-    stage1(3)
     stage2(2)
-    stage3(0)
-    product(5, s["gpre"], s["normed"])
-    rs_copy(5, 0).start()
-    stage1(4)
-    ar_start(2, ar_sum(1))
-    stage3(1)
-    stage1(5)
-    stage3(2)
-    total = finish(0)
-    hall[core, h1, h2, h3] = total[:, 128:256]
+    stage2(3)
+    finish(0)
     ag_start(0)
-    finish(1)
-    finish(2)
-    ar_start(3, ar_sum(2))
-    ag_wait(0)
-    ag_start(1)
-    stage2(3)
-    stage2(4)
-    stage2(5)
-    ag_wait(1)
-    ag_start(2)
-    sums = ar_sum(3)
-    conv_out[...] = sums[0:9]
-    gain_out[...] = sums[9:10]
-    stage3(3)
-    stage3(4)
-    stage3(5)
-    ag_wait(2)
-    ag_start(3)
-    finish(3)
-    finish(4)
-    finish(5)
-    ag_wait(3)
-    for t in range(HEAD_TILES):
-        i1, i2, i3 = spot(0, t // 64, (t // 16) % 4, (t // 8) % 2, (t // 2) % 4)
-        rt, ct = t // 3, t % 3
-        n = min(128, OUTC - ct * 128)
-        head_out[rt * 16 : rt * 16 + 16, ct * 128 : ct * 128 + n] = hall[t % 2, i1, i2, i3, :, 0:n]
+    stage1(6)
 
     @pl.loop(0, LATD)
     def _(ci):
@@ -570,16 +617,59 @@
             y_copy(ci, k).wait_send()
             g_copy(ci, k).wait_send()
 
-    for k in range(6):
-        rs_copy(k, 0).wait_send()
-        for stage in (1, 2, 3):
-            for j in (1, 2, 3):
-                rs_copy(k, stage, j).wait_send()
+    stage3(1)
+    ag_wait(0)
+    ag_start(1)
+    sent(0, 1)
+    stage2(4)
+    ar_start(2, ar_sum(1))
+    stage3(3)
+    stage3(2)
+    stage2(5)
+    ag_wait(1)
+    ag_start(2)
+    stage2(6)
+    finish(1)
+    finish(3)
+    finish(2)
+    out_cp[1].start()
+    sent(2)
+    stage3(4)
+    ar_start(3, ar_sum(2))
+    stage3(6)
+    stage3(5)
+    ag_wait(2)
+    ag_start(3)
+    finish(4)
+    finish(6)
+    finish(5)
+    out_cp[0].start()
+    ag_wait(3)
+    for t in range(HEAD_TILES):
+        i1, i2, i3 = spot(0, t // 64, (t // 16) % 4, (t // 8) % 2, (t // 2) % 4)
+        rt, ct = t // 5, t % 5
+        s["o_head"][rt * 16 : rt * 16 + 16, ct * 128 : ct * 128 + 128] = hall[t % 2, i1, i2, i3].astype(F32)
+
+    out_cp[2].start()
+    sums = ar_sum(3)
+    s["o_conv"][...] = sums[0:9]
+    s["o_gain"][...] = sums[9, :]
+    out_cp[3].start()
+    out_cp[4].start()
+
+    sent(3)
     for n in range(4):
         for j in (1,) if n == 3 else (1, 2, 3):
             ag_copy(n, j).wait_send()
         for j in (1,) if n == 0 else (1, 2, 3):
             ar_copy(n, j).wait_send()
+    for cp in out_cp:
+        cp.wait()
+
+
+def hand_on(*refs):
+    for k in range(5):
+        refs[5 + k][...] = refs[k][...]
 
 
 def body(
@@ -587,18 +677,18 @@
 ):
     vmem = pl.BlockSpec(memory_space=pltpu.VMEM)
     hbm = pl.BlockSpec(memory_space=pl.ANY)
-    gin, gdn, head, gain, conv = pl.pallas_call(
+    parts = pl.pallas_call(
         kernel,
         name="ensemble_block",
         out_shape=(
             jax.ShapeDtypeStruct((15, D), F32),
             jax.ShapeDtypeStruct((15, D), F32),
-            jax.ShapeDtypeStruct((D, OUTC), F32),
-            jax.ShapeDtypeStruct((1, D), F32),
+            jax.ShapeDtypeStruct((OUTC, D), F32),
+            jax.ShapeDtypeStruct((D,), F32),
             jax.ShapeDtypeStruct((9, D), F32),
         ),
-        in_specs=[hbm, hbm, vmem, vmem, hbm, hbm, hbm, hbm],
-        out_specs=(vmem,) * 5,
+        in_specs=[hbm] * 8,
+        out_specs=(hbm,) * 5,
         scratch_shapes=list(scratch().values()),
         compiler_params=pltpu.CompilerParams(
             collective_id=0, has_side_effects=True, vmem_limit_bytes=62 * 2**20
@@ -607,10 +697,24 @@
             flops=17_000_000_000, bytes_accessed=9_000_000, transcendentals=2_100_000
         ),
     )(
-        latent_state, member_noise, conv_weight, norm_gain.reshape(1, D), weight_in, weight_down,
-        weight_head, target_field,
+        latent_state, member_noise, conv_weight, norm_gain, weight_in, weight_down,
+        weight_head.T, jnp.swapaxes(target_field, 1, 2),
     )
-    return gin, gdn, head, gain.reshape(D), conv
+    gin, gdn, head, gain, conv = pl.pallas_call(
+        hand_on,
+        name="hand_on",
+        out_shape=(
+            jax.ShapeDtypeStruct((15, D), F32),
+            jax.ShapeDtypeStruct((15, D), F32),
+            jax.ShapeDtypeStruct((OUTC, D), F32),
+            jax.ShapeDtypeStruct((D,), F32),
+            jax.ShapeDtypeStruct((9, D), F32),
+        ),
+        in_specs=[vmem] * 5,
+        out_specs=(vmem,) * 5,
+        cost_estimate=pl.CostEstimate(flops=0, bytes_accessed=1_900_000, transcendentals=0),
+    )(*parts)
+    return gin, gdn, head.T, gain, conv
 
 
 def solution(mesh):

time: 101 us -> 82.5 us (0.82)
  local copies, waits for them, and re-layouts: 12.1 us -> 0 us
  Pallas kernels: 86.5 us -> 81.7 us
  other arithmetic: 1.27 us -> 0 us
    unnamed x6 -> x0, local copies, waits for them, and re-layouts: 10.8 us -> none
    pallas_call x1, Pallas kernels: 86.5 us -> 79.5 us  [body(): pl.pallas_call(kernel, name='ensemble_block', out_shape=(jax.ShapeDtypeSt...]
    pallas_call x0 -> x1, Pallas kernels: none -> 2.16 us  [body(): pl.pallas_call(hand_on, name='hand_on', out_shape=(jax.ShapeDtypeStruct((...]
    pallas_call x1 -> x0, other arithmetic: 1.27 us -> none  [body(): pl.pallas_call(kernel, name='ensemble_block', out_shape=(jax.ShapeDtypeSt...]
    reshape x1 -> x0, local copies, waits for them, and re-layouts: 1.27 us -> none  [body(): norm_gain.reshape(1, D)]
where the time goes in v1:
time: 82.5 us; the launch traced here: 82.3 us
  Pallas kernels  81.7 us (99%)
    pallas_call x1, Pallas kernels, body(): pl.pallas_call(kernel, name='ensemble_block', out_shape=(jax.ShapeDtypeSt...  79.5 us
    pallas_call x1, Pallas kernels, body(): pl.pallas_call(hand_on, name='hand_on', out_shape=(jax.ShapeDtypeStruct((...  2.16 us

profile of v1, /device:TPU:1, one launch (start us, length us, event | category | flops | bytes accessed | tf_op | source)
XLA Modules:
  0.0 82.3 jit_solution(17461602550180395048)
XLA Ops:
  0.6 79.5 %ensemble_block.1 = (f32[15,640]{1,0:T(8,128)}, f32[15,640]{1,0:T(8,128)}, f32[320,640]{1,0:T(8,128)}, f32[640]{0:T(1024)}, f32[9,640]{1,0:T(8,128)}) custom-call(bf16[4,128,640]{2,1,0:T(8,128)(2,1)} %lat_hbm.1, bf16[2,4,128,640]{3,2,1,0:T(8,128)(2,1)} %noise_hbm.1, f32[9,640]{1,0:T(8,128)} %cw_hbm.1, f32[640]{0:T(1024)} %gain_hbm.1, ...), custom_call_target="tpu_custom_call" | custom-call | flops 16999999488 | bytes 9000000 | tf_op jit(solution)/shard_map/ensemble_block/pallas_call | solution.py:680
  80.2 2.2 %hand_on.1 = (f32[15,640]{1,0:T(8,128)}, f32[15,640]{1,0:T(8,128)}, f32[320,640]{1,0:T(8,128)}, f32[640]{0:T(1024)}, f32[9,640]{1,0:T(8,128)}) custom-call(f32[15,640]{1,0:T(8,128)} %get-tuple-element.15.refs_0_, f32[15,640]{1,0:T(8,128)} %get-tuple-element.16.refs_1_, f32[320,640]{1,0:T(8,128)} %get-tuple-element.17.refs_2_, ...), custom_call_target="tpu_custom_call" | custom-call | bytes 1900000 | tf_op jit(solution)/shard_map/hand_on/pallas_call | solution.py:703

commit v2 on v1

--- a/solution.py
+++ b/solution.py
@@ -71,7 +71,6 @@
         "gain": pltpu.VMEM((D,), F32),
         "o_gin": pltpu.VMEM((15, D), F32),
         "o_gdn": pltpu.VMEM((15, D), F32),
-        "o_head": pltpu.VMEM((OUTC, D), F32),
         "o_gain": pltpu.VMEM((D,), F32),
         "o_conv": pltpu.VMEM((9, D), F32),
         "o_sem": pltpu.SemaphoreType.DMA((5,)),
@@ -192,7 +191,7 @@
             (
                 ("o_gin", gin_hbm),
                 ("o_gdn", gdn_hbm),
-                ("o_head", head_hbm),
+                ("hall", head_hbm),
                 ("o_gain", ggain_hbm),
                 ("o_conv", gconv_hbm),
             )
@@ -362,9 +361,9 @@
         for k in range(7):
             y_copy(ci, k).start()
 
-        @pl.when(ci > 0)
+        @pl.when(ci > 1)
         def _():
-            score(ci - 1)
+            score(ci - 2)
 
     def order(k):
         return CHUNKS[k][3]
@@ -557,9 +556,9 @@
 
     @pl.loop(0, 3)
     def _(ci):
-        @pl.when(ci == 2)
+        @pl.when(ci < 2)
         def _():
-            score(LATD - 1)
+            score(ci + 2)
 
         grad_hidden(ci, 1)
         grad_act(ci, 1)
@@ -590,26 +589,26 @@
     stage1(2)
     grad_act(3, 1)
     stage1(3)
-    stage2(0)
     product(4, gpre, normed)
     send0(4)
+    stage2(0)
     product(5, gpre, normed)
     send0(5)
     stage1(4)
+    product(6, gpre, normed)
+    send0(6)
+    stage1(5)
     stage3(0)
     grad_normed(3, 1)
-    stage1(5)
+    stage1(6)
     stage2(1)
+    stage2(2)
     conv_back(3, 0)
     ar_start(0, jnp.sum(s["cacc"][...], axis=1))
-    product(6, gpre, normed)
-    send0(6)
+    stage2(3)
     ar_start(1, ar_sum(0))
-    stage2(2)
-    stage2(3)
     finish(0)
     ag_start(0)
-    stage1(6)
 
     @pl.loop(0, LATD)
     def _(ci):
@@ -618,38 +617,33 @@
             g_copy(ci, k).wait_send()
 
     stage3(1)
+    stage3(2)
     ag_wait(0)
     ag_start(1)
-    sent(0, 1)
+    stage3(3)
     stage2(4)
+    stage2(5)
     ar_start(2, ar_sum(1))
-    stage3(3)
-    stage3(2)
-    stage2(5)
+    stage2(6)
     ag_wait(1)
     ag_start(2)
-    stage2(6)
     finish(1)
+    finish(2)
     finish(3)
-    finish(2)
     out_cp[1].start()
-    sent(2)
     stage3(4)
+    stage3(5)
     ar_start(3, ar_sum(2))
     stage3(6)
-    stage3(5)
     ag_wait(2)
     ag_start(3)
+    sent(0, 1)
+    sent(2)
     finish(4)
+    finish(5)
     finish(6)
-    finish(5)
     out_cp[0].start()
     ag_wait(3)
-    for t in range(HEAD_TILES):
-        i1, i2, i3 = spot(0, t // 64, (t // 16) % 4, (t // 8) % 2, (t // 2) % 4)
-        rt, ct = t // 5, t % 5
-        s["o_head"][rt * 16 : rt * 16 + 16, ct * 128 : ct * 128 + 128] = hall[t % 2, i1, i2, i3].astype(F32)
-
     out_cp[2].start()
     sums = ar_sum(3)
     s["o_conv"][...] = sums[0:9]
@@ -667,9 +661,16 @@
         cp.wait()
 
 
-def hand_on(*refs):
-    for k in range(5):
-        refs[5 + k][...] = refs[k][...]
+def hand_on(gin, gdn, tiles, gain, conv, gin_out, gdn_out, head_out, gain_out, conv_out):
+    gin_out[...] = gin[...]
+    gdn_out[...] = gdn[...]
+    for t in range(HEAD_TILES):
+        v = {"x": (t // 2) % 4, "y": (t // 8) % 2 * 2 + t // 64, "z": (t // 16) % 4}
+        i1, i2, i3 = (v[a] for a in CHUNKS[0][3])
+        rt, ct = t // 5, t % 5
+        head_out[rt * 16 : rt * 16 + 16, ct * 128 : ct * 128 + 128] = tiles[t % 2, i1, i2, i3].astype(F32)
+    gain_out[...] = gain[...]
+    conv_out[...] = conv[...]
 
 
 def body(
@@ -683,7 +684,7 @@
         out_shape=(
             jax.ShapeDtypeStruct((15, D), F32),
             jax.ShapeDtypeStruct((15, D), F32),
-            jax.ShapeDtypeStruct((OUTC, D), F32),
+            jax.ShapeDtypeStruct((2, 4, 4, 4, 16, 128), BF),
             jax.ShapeDtypeStruct((D,), F32),
             jax.ShapeDtypeStruct((9, D), F32),
         ),

time: 82.5 us -> 80.5 us (0.976)
  Pallas kernels: 81.7 us -> 79.7 us
    pallas_call x1, Pallas kernels: 79.5 us -> 77.7 us  [body(): pl.pallas_call(kernel, name='ensemble_block', out_shape=(jax.ShapeDtypeSt...]
where the time goes in v2:
time: 80.5 us; the launch traced here: 80.4 us
  Pallas kernels  79.7 us (99%)
    pallas_call x1, Pallas kernels, body(): pl.pallas_call(kernel, name='ensemble_block', out_shape=(jax.ShapeDtypeSt...  77.7 us
    pallas_call x1, Pallas kernels, body(): pl.pallas_call(hand_on, name='hand_on', out_shape=(jax.ShapeDtypeStruct((...  2.06 us

profile of v2, /device:TPU:1, one launch (start us, length us, event | category | flops | bytes accessed | tf_op | source)
XLA Modules:
  0.0 80.4 jit_solution(4020546065694875830)
XLA Ops:
  0.6 77.7 %ensemble_block.1 = (f32[15,640]{1,0:T(8,128)}, f32[15,640]{1,0:T(8,128)}, bf16[2,4,4,4,16,128]{5,4,3,2,1,0:T(8,128)(2,1)}, f32[640]{0:T(1024)}, f32[9,640]{1,0:T(8,128)}) custom-call(bf16[4,128,640]{2,1,0:T(8,128)(2,1)} %lat_hbm.1, bf16[2,4,128,640]{3,2,1,0:T(8,128)(2,1)} %noise_hbm.1, f32[9,640]{1,0:T(8,128)} %cw_hbm.1, f32[640]{0:T(1024)} %gain_hbm.1, ...), custom_call_target="tpu_custom_call" | custom-call | flops 16999999488 | bytes 9000000 | tf_op jit(solution)/shard_map/ensemble_block/pallas_call | solution.py:681
  78.3 2.1 %hand_on.1 = (f32[15,640]{1,0:T(8,128)}, f32[15,640]{1,0:T(8,128)}, f32[320,640]{1,0:T(8,128)}, f32[640]{0:T(1024)}, f32[9,640]{1,0:T(8,128)}) custom-call(f32[15,640]{1,0:T(8,128)} %get-tuple-element.15.gin, f32[15,640]{1,0:T(8,128)} %get-tuple-element.16.gdn, bf16[2,4,4,4,16,128]{5,4,3,2,1,0:T(8,128)(2,1)} %get-tuple-element.17.tiles, ...), custom_call_target="tpu_custom_call" | custom-call | bytes 1900000 | tf_op jit(solution)/shard_map/hand_on/pallas_call | solution.py:704

commit v3 on v2

--- a/solution.py
+++ b/solution.py
@@ -357,9 +357,12 @@
                 mixed[5] = jnp.zeros((MEM, LON, D), BF)
 
         mixer(ci)
-        conv_norm(ci + 1)
         for k in range(7):
             y_copy(ci, k).start()
+
+        @pl.when(ci < LATD - 1)
+        def _():
+            conv_norm(ci + 1)
 
         @pl.when(ci > 1)
         def _():
@@ -601,10 +604,10 @@
     stage3(0)
     grad_normed(3, 1)
     stage1(6)
+    conv_back(3, 0)
+    ar_start(0, jnp.sum(s["cacc"][...], axis=1))
     stage2(1)
     stage2(2)
-    conv_back(3, 0)
-    ar_start(0, jnp.sum(s["cacc"][...], axis=1))
     stage2(3)
     ar_start(1, ar_sum(0))
     finish(0)

time: 80.5 us -> 79.9 us (level)
  no operation moved by 1% of the time
where the time goes in v3:
time: 79.9 us; the launch traced here: 79.7 us
  Pallas kernels  79.1 us (99%)
    pallas_call x1, Pallas kernels, body(): pl.pallas_call(kernel, name='ensemble_block', out_shape=(jax.ShapeDtypeSt...  77 us
    pallas_call x1, Pallas kernels, body(): pl.pallas_call(hand_on, name='hand_on', out_shape=(jax.ShapeDtypeStruct((...  2.06 us

profile of v3, /device:TPU:1, one launch (start us, length us, event | category | flops | bytes accessed | tf_op | source)
XLA Modules:
  0.0 79.7 jit_solution(17096814974036535387)
XLA Ops:
  0.6 77.0 %ensemble_block.1 = (f32[15,640]{1,0:T(8,128)}, f32[15,640]{1,0:T(8,128)}, bf16[2,4,4,4,16,128]{5,4,3,2,1,0:T(8,128)(2,1)}, f32[640]{0:T(1024)}, f32[9,640]{1,0:T(8,128)}) custom-call(bf16[4,128,640]{2,1,0:T(8,128)(2,1)} %lat_hbm.1, bf16[2,4,128,640]{3,2,1,0:T(8,128)(2,1)} %noise_hbm.1, f32[9,640]{1,0:T(8,128)} %cw_hbm.1, f32[640]{0:T(1024)} %gain_hbm.1, ...), custom_call_target="tpu_custom_call" | custom-call | flops 16999999488 | bytes 9000000 | tf_op jit(solution)/shard_map/ensemble_block/pallas_call | solution.py:684
  77.7 2.1 %hand_on.1 = (f32[15,640]{1,0:T(8,128)}, f32[15,640]{1,0:T(8,128)}, f32[320,640]{1,0:T(8,128)}, f32[640]{0:T(1024)}, f32[9,640]{1,0:T(8,128)}) custom-call(f32[15,640]{1,0:T(8,128)} %get-tuple-element.15.gin, f32[15,640]{1,0:T(8,128)} %get-tuple-element.16.gdn, bf16[2,4,4,4,16,128]{5,4,3,2,1,0:T(8,128)(2,1)} %get-tuple-element.17.tiles, ...), custom_call_target="tpu_custom_call" | custom-call | bytes 1900000 | tf_op jit(solution)/shard_map/hand_on/pallas_call | solution.py:707
